TPU v7x, 32 devices: a whole 2x2x4 slice. The times are simulated.
32 devices in a mesh: dp: 4 (over y, core), loop: 8 (over z, x).
Axes of the slice: x: 2, y: 2, z: 4, core: 2. Of those that a mesh axis runs over, the one named last changes fastest.
Arguments:
- image_embeds: bfloat16 [4096, 1152], P(('dp', 'loop')), may hold values from -0.6 to 0.6
- text_embeds: bfloat16 [4096, 1152], P(('dp', 'loop')), may hold values from -0.6 to 0.6
- log_scale: float32 [1], replicated, may hold values from 2 to 2.7
- logit_bias: float32 [1], replicated, may hold values from -8 to -5
Outputs:
- loss: float32 [1], replicated
- image_grad: bfloat16 [4096, 1152], P(('dp', 'loop'))
- text_grad: bfloat16 [4096, 1152], P(('dp', 'loop'))
- grad_log_scale: float32 [1], replicated
- grad_bias: float32 [1], replicated
All inputs are finite; a program needn't handle non-finite values.
Results may differ from a plain program's by a relative error of at most 0.0065.
Values may be sent and summed in bfloat16 or wider, within the bound.
A program may use at most 64 MiB of HBM per device.

v0:
```python
import functools

import jax
import jax.numpy as jnp
from jax import lax
from jax.experimental import pallas as pl
from jax.experimental.pallas import tpu as pltpu
from jax.sharding import PartitionSpec as P

EPSILON = 1e-06
TEXT, IMAGE = 0, 1
CUTS = ((0, 4, 8), (0, 5, 8))
CHUNKS = tuple(len(cuts) - 1 for cuts in CUTS)


def inverse_norm(floats):
    return lax.rsqrt(jnp.sum(floats * floats, axis=1, keepdims=True) + EPSILON)


def softplus_and_sigmoid(logits):
    small = jnp.exp(-jnp.abs(logits))
    softplus = jnp.maximum(logits, 0.0) + jnp.log1p(small)
    sigmoid = jnp.where(logits >= 0.0, 1.0, small) / (1.0 + small)
    return softplus, sigmoid


def dot_nt(left, right):
    return lax.dot_general(
        left, right, (((1,), (1,)), ((), ())), preferred_element_type=jnp.float32
    )


def unit_pull(embeds, r, cot, temper):
    floats = embeds.astype(jnp.float32)
    along = jnp.sum(floats * cot, axis=1, keepdims=True)
    return ((temper * r) * (cot - floats * (r * r * along))).astype(jnp.bfloat16)


def kernel(
    n_dp, n_loop,
    image_hbm, text_hbm, scale_ref, bias_ref,
    image_grad_ref, text_grad_ref, sums_ref,
    raw, own_image, units, total, norms, dp_sums, loop_sums,
    load_sem, send_sem, recv_sem, pass_sem, sum_send, sum_recv,
):
    rows = own_image.shape[0]
    chips = n_dp // 2
    dp, loop = lax.axis_index("dp"), lax.axis_index("loop")
    core = lax.rem(dp, 2)
    sibling = dp + 1 - 2 * core

    def peer_dp(step):
        return lax.rem(dp + step, n_dp)

    def peer_loop(step):
        return lax.rem(loop + step, n_loop)

    barrier = pltpu.get_barrier_semaphore()
    for step in range(1, n_dp):
        pl.semaphore_signal(barrier, inc=1, device_id={"dp": peer_dp(step)}, device_id_type=pl.DeviceIdType.MESH)
    for step in range(1, n_loop):
        pl.semaphore_signal(barrier, inc=1, device_id={"loop": peer_loop(step)}, device_id_type=pl.DeviceIdType.MESH)

    loads = [
        pltpu.make_async_copy(text_hbm, raw.at[0], load_sem.at[TEXT]),
        pltpu.make_async_copy(image_hbm, own_image, load_sem.at[IMAGE]),
    ]
    for load in loads:
        load.start()

    def normalize(kind, slot, embeds):
        floats = embeds.astype(jnp.float32)
        r = inverse_norm(floats)
        units[kind, slot] = (floats * r).astype(jnp.bfloat16)
        return r

    def piece(kind, part):
        first, last = CUTS[kind][part] * rows // 8, CUTS[kind][part + 1] * rows // 8
        return pl.ds(first, last - first)

    def block(kind, slot):
        return raw.at[slot] if kind == TEXT else units.at[IMAGE, slot]

    def copy(kind, part, source, to_slot, target, sem):
        return pltpu.make_async_remote_copy(
            src_ref=source.at[piece(kind, part)],
            dst_ref=block(kind, to_slot).at[piece(kind, part)],
            send_sem=sem.at[kind, to_slot, part],
            recv_sem=recv_sem.at[kind, to_slot, part],
            device_id={"dp": target},
            device_id_type=pl.DeviceIdType.MESH,
        )

    sources = (text_hbm, units.at[IMAGE, 0])
    sent = []

    def send(kind, part):
        copies = [copy(kind, part, sources[kind], 2 * k, peer_dp(2 * k), send_sem) for k in range(1, chips)]
        for c in copies:
            c.start()
        return copies

    def send_sibling(kind):
        for part in range(CHUNKS[kind]):
            sent.append(copy(kind, part, sources[kind], 1, sibling, send_sem))
            sent[-1].start()

    def leave(copies):
        for c in copies:
            c.wait_send()

    def arrival(kind, part, slot):
        return copy(kind, part, sources[kind], slot, sibling, send_sem)

    def pass_on(kind, part):
        for k in range(1, chips):
            arrival(kind, part, 2 * k).wait_recv()
            sent.append(copy(kind, part, block(kind, 2 * k), 2 * k + 1, sibling, pass_sem))
            sent[-1].start()

    pl.semaphore_wait(barrier, n_dp + n_loop - 2)
    texts_out = [c for part in range(CHUNKS[TEXT]) for c in send(TEXT, part)]
    send_sibling(TEXT)
    loads[IMAGE].wait()
    norms[IMAGE] = normalize(IMAGE, 0, own_image[...])
    send_sibling(IMAGE)
    loads[TEXT].wait()
    norms[TEXT] = normalize(TEXT, 0, raw[0])

    temper = jnp.exp(jnp.full((1, 128), scale_ref[0], jnp.float32))[:, :1]
    offset = bias_ref[0]
    image_unit = units[IMAGE, 0]
    text_unit = units[TEXT, 0]

    def eye():
        ids = lax.broadcasted_iota(jnp.int32, (rows, rows), 0)
        return ids == lax.broadcasted_iota(jnp.int32, (rows, rows), 1)

    sums = [jnp.zeros((rows, 128), jnp.float32) for _ in range(3)]

    def folded(values):
        return sum(values[:, c:c + 128] for c in range(0, values.shape[1], 128))

    def less_eye(values, subtrahend):
        wide = jnp.concatenate([eye(), jnp.zeros((rows, rows), jnp.bool_)], axis=1)
        return jnp.where(wide, values - subtrahend, values)

    def row_pair(k, first):
        texts = units[TEXT, 2 * k:2 * k + 2].reshape(2 * rows, -1)
        scaled = temper * dot_nt(image_unit, texts)
        logits = scaled + offset
        losses, coef = softplus_and_sigmoid(logits)
        if first:
            losses = less_eye(losses, logits)
            coef = less_eye(coef, 1.0)
        for i, values in enumerate((losses, coef * scaled, coef)):
            sums[i] += folded(values)
        return jnp.dot(coef.astype(jnp.bfloat16), texts, preferred_element_type=jnp.float32)

    def col_part(images, first):
        logits = temper * dot_nt(text_unit, images) + offset
        _, coef = softplus_and_sigmoid(logits)
        if first:
            coef = less_eye(coef, 1.0)
        return jnp.dot(coef.astype(jnp.bfloat16), images, preferred_element_type=jnp.float32)

    def image_pair(k, part):
        return units[IMAGE, 2 * k:2 * k + 2, piece(IMAGE, part)].reshape(-1, units.shape[3])

    for part in range(CHUNKS[TEXT]):
        arrival(TEXT, part, 1).wait_recv()
    normalize(TEXT, 1, raw[1])
    total[IMAGE] = row_pair(0, True)
    for part in range(CHUNKS[IMAGE]):
        arrival(IMAGE, part, 1).wait_recv()
    total[TEXT] = col_part(units[IMAGE, 0:2].reshape(2 * rows, -1), True)
    leave(texts_out)
    images_out = [c for part in range(CHUNKS[IMAGE]) for c in send(IMAGE, part)]
    for part in range(CHUNKS[TEXT]):
        pass_on(TEXT, part)
    for k in range(1, chips):
        normalize(TEXT, 2 * k, raw[2 * k])
        for part in range(CHUNKS[TEXT]):
            arrival(TEXT, part, 2 * k + 1).wait_recv()
        normalize(TEXT, 2 * k + 1, raw[2 * k + 1])
        total[IMAGE] += row_pair(k, False)

    def exchange(stage, buffer, count, target, axis):
        copies = []
        for step in range(1, count):
            copies.append(pltpu.make_async_remote_copy(
                src_ref=buffer.at[0],
                dst_ref=buffer.at[step],
                send_sem=sum_send.at[stage, step],
                recv_sem=sum_recv.at[stage, step],
                device_id={axis: target(step)},
                device_id_type=pl.DeviceIdType.MESH,
            ))
            copies[-1].start()
        return copies

    dp_sums[0] = jnp.concatenate(
        [jnp.sum(s, axis=0, keepdims=True) for s in sums] + [jnp.zeros((5, 128), jnp.float32)], axis=0
    )
    dp_copies = exchange(0, dp_sums, n_dp, peer_dp, "dp")

    image_grad_ref[...] = unit_pull(own_image[...], norms[IMAGE], total[IMAGE], temper)

    pass_on(IMAGE, 0)
    for c in dp_copies:
        c.wait_recv()
    loop_sums[0] = jnp.sum(dp_sums[...], axis=0)
    loop_copies = exchange(1, loop_sums, n_loop, peer_loop, "loop")
    for part in range(CHUNKS[IMAGE] - 1):
        for k in range(1, chips):
            arrival(IMAGE, part, 2 * k + 1).wait_recv()
            total[TEXT] += col_part(image_pair(k, part), False)
        pass_on(IMAGE, part + 1)
    last = CHUNKS[IMAGE] - 1
    for k in range(1, chips):
        total[TEXT] += col_part(units[IMAGE, 2 * k, piece(IMAGE, last)], False)
    for k in range(1, chips):
        arrival(IMAGE, last, 2 * k + 1).wait_recv()
        total[TEXT] += col_part(units[IMAGE, 2 * k + 1, piece(IMAGE, last)], False)
    text_grad_ref[...] = unit_pull(raw[0], norms[TEXT], total[TEXT], temper)

    for c in loop_copies:
        c.wait_recv()
    sums_ref[...] = jnp.sum(loop_sums[...], axis=0)

    leave(sent + images_out + dp_copies + loop_copies)


def finish(
    inverse_batch, image_grad, text_grad, sums_ref,
    loss_ref, image_grad_hbm, text_grad_hbm, scale_grad_ref, bias_grad_ref, sems,
):
    stores = [
        pltpu.make_async_copy(image_grad, image_grad_hbm, sems.at[0]),
        pltpu.make_async_copy(text_grad, text_grad_hbm, sems.at[1]),
    ]
    for store in stores:
        store.start()
    loss_ref[0] = jnp.sum(sums_ref[0:1, :]) * inverse_batch
    scale_grad_ref[0] = jnp.sum(sums_ref[1:2, :])
    bias_grad_ref[0] = jnp.sum(sums_ref[2:3, :])
    for store in stores:
        store.wait()


def solution(mesh):
    n_dp, n_loop = mesh.shape["dp"], mesh.shape["loop"]

    def on_device(image_embeds, text_embeds, log_scale, logit_bias):
        rows, width = image_embeds.shape
        scalar = jax.ShapeDtypeStruct((1,), jnp.float32)
        grad = jax.ShapeDtypeStruct((rows, width), jnp.bfloat16)
        hbm = pl.BlockSpec(memory_space=pltpu.HBM)
        vmem = pl.BlockSpec(memory_space=pltpu.VMEM)
        smem = pl.BlockSpec(memory_space=pltpu.SMEM)
        parts = max(CHUNKS)
        image_grad, text_grad, sums = pl.pallas_call(
            functools.partial(kernel, n_dp, n_loop),
            out_shape=(
                pltpu.VMEM((rows, width), jnp.bfloat16),
                pltpu.VMEM((rows, width), jnp.bfloat16),
                pltpu.VMEM((8, 128), jnp.float32),
            ),
            in_specs=[hbm, hbm, smem, smem],
            out_specs=(vmem, vmem, vmem),
            scratch_shapes=[
                pltpu.VMEM((n_dp, rows, width), jnp.bfloat16),
                pltpu.VMEM((rows, width), jnp.bfloat16),
                pltpu.VMEM((2, n_dp, rows, width), jnp.bfloat16),
                pltpu.VMEM((2, rows, width), jnp.float32),
                pltpu.VMEM((2, rows, 1), jnp.float32),
                pltpu.VMEM((n_dp, 8, 128), jnp.float32),
                pltpu.VMEM((n_loop, 8, 128), jnp.float32),
                pltpu.SemaphoreType.DMA((2,)),
                pltpu.SemaphoreType.DMA((2, n_dp, parts)),
                pltpu.SemaphoreType.DMA((2, n_dp, parts)),
                pltpu.SemaphoreType.DMA((2, n_dp, parts)),
                pltpu.SemaphoreType.DMA((2, max(n_dp, n_loop))),
                pltpu.SemaphoreType.DMA((2, max(n_dp, n_loop))),
            ],
            compiler_params=pltpu.CompilerParams(
                collective_id=0, has_side_effects=True, vmem_limit_bytes=32 * 1024 * 1024
            ),
        )(
            pltpu.with_memory_space_constraint(image_embeds, pltpu.HBM),
            pltpu.with_memory_space_constraint(text_embeds, pltpu.HBM),
            log_scale,
            logit_bias,
        )
        return pl.pallas_call(
            functools.partial(finish, 1.0 / (rows * n_dp * n_loop)),
            out_shape=(scalar, grad, grad, scalar, scalar),
            in_specs=[vmem] * 3,
            out_specs=(smem, hbm, hbm, smem, smem),
            scratch_shapes=[pltpu.SemaphoreType.DMA((2,))],
            compiler_params=pltpu.CompilerParams(vmem_limit_bytes=4 * 1024 * 1024),
        )(image_grad, text_grad, sums)

    return jax.shard_map(
        on_device,
        mesh=mesh,
        in_specs=(P(("dp", "loop"), None), P(("dp", "loop"), None), P(), P()),
        out_specs=(P(), P(("dp", "loop"), None), P(("dp", "loop"), None), P(), P()),
        check_vma=False,
    )
```

profile of v0, /device:TPU:0, one launch (start us, length us, event | category | flops | bytes accessed | tf_op | source)
XLA Modules:
  0.0 27.8 jit_solution(1419743042662396176)
XLA Ops:
  1.9 24.5 %shard_map.83 = (bf16[128,1152]{1,0:T(8,128)(2,1)S(1)}, bf16[128,1152]{1,0:T(8,128)(2,1)S(1)}, f32[8,128]{1,0:T(8,128)S(1)}) custom-call(bf16[128,1152]{1,0:T(8,128)(2,1)} %image_hbm.1, bf16[128,1152]{1,0:T(8,128)(2,1)} %text_hbm.1, f32[1]{0:T(128)S(6)} %copy.9.scale_ref, f32[1]{0:T(128)S(6)} %copy.10.bias_ref), custom_call_target="tpu_custom_call" | custom-call | tf_op jit(solution)/shard_map/pallas_call | solution.py:262
  26.4 1.4 %shard_map.84 = (f32[1]{0:T(128)}, bf16[128,1152]{1,0:T(8,128)(2,1)}, bf16[128,1152]{1,0:T(8,128)(2,1)}, f32[1]{0:T(128)}, f32[1]{0:T(128)}) custom-call(bf16[128,1152]{1,0:T(8,128)(2,1)S(1)} %get-tuple-element.8.image_grad, bf16[128,1152]{1,0:T(8,128)(2,1)S(1)} %get-tuple-element.9.text_grad, f32[8,128]{1,0:T(8,128)S(1)} %get-tuple-element.10.sums_ref), custom_call_target="tpu_custom_call" | custom-call | tf_op jit(solution)/shard_map/pallas_call | solution.py:295
where the time goes:
time: 27.9 us; the launch traced here: 27.8 us
  Pallas kernels  25.8 us (92%)
  between operations  1.93 us (7%)
    pallas_call x1, Pallas kernels, on_device(): pl.pallas_call(functools.partial(kernel, n_dp, n_loop), out_shape=(pltpu....  24.5 us
    pallas_call x1, Pallas kernels, on_device(): pl.pallas_call(functools.partial(finish, 1.0 / (rows * n_dp * n_loop)), o...  1.36 us

commit v1 on v0

--- a/solution.py
+++ b/solution.py
@@ -40,10 +40,10 @@
     n_dp, n_loop,
     image_hbm, text_hbm, scale_ref, bias_ref,
     image_grad_ref, text_grad_ref, sums_ref,
-    raw, own_image, units, total, norms, dp_sums, loop_sums,
+    own, units, total, norms, dp_sums, loop_sums,
     load_sem, send_sem, recv_sem, pass_sem, sum_send, sum_recv,
 ):
-    rows = own_image.shape[0]
+    rows = own.shape[1]
     chips = n_dp // 2
     dp, loop = lax.axis_index("dp"), lax.axis_index("loop")
     core = lax.rem(dp, 2)
@@ -62,47 +62,44 @@
         pl.semaphore_signal(barrier, inc=1, device_id={"loop": peer_loop(step)}, device_id_type=pl.DeviceIdType.MESH)
 
     loads = [
-        pltpu.make_async_copy(text_hbm, raw.at[0], load_sem.at[TEXT]),
-        pltpu.make_async_copy(image_hbm, own_image, load_sem.at[IMAGE]),
+        pltpu.make_async_copy(text_hbm, own.at[TEXT], load_sem.at[TEXT]),
+        pltpu.make_async_copy(image_hbm, own.at[IMAGE], load_sem.at[IMAGE]),
     ]
     for load in loads:
         load.start()
 
-    def normalize(kind, slot, embeds):
-        floats = embeds.astype(jnp.float32)
+    def normalize(kind):
+        loads[kind].wait()
+        floats = own[kind].astype(jnp.float32)
         r = inverse_norm(floats)
-        units[kind, slot] = (floats * r).astype(jnp.bfloat16)
-        return r
+        units[kind, 0] = (floats * r).astype(jnp.bfloat16)
+        norms[kind] = r
 
     def piece(kind, part):
         first, last = CUTS[kind][part] * rows // 8, CUTS[kind][part + 1] * rows // 8
         return pl.ds(first, last - first)
 
-    def block(kind, slot):
-        return raw.at[slot] if kind == TEXT else units.at[IMAGE, slot]
-
-    def copy(kind, part, source, to_slot, target, sem):
+    def copy(kind, part, from_slot, to_slot, target, sem):
         return pltpu.make_async_remote_copy(
-            src_ref=source.at[piece(kind, part)],
-            dst_ref=block(kind, to_slot).at[piece(kind, part)],
+            src_ref=units.at[kind, from_slot, piece(kind, part)],
+            dst_ref=units.at[kind, to_slot, piece(kind, part)],
             send_sem=sem.at[kind, to_slot, part],
             recv_sem=recv_sem.at[kind, to_slot, part],
             device_id={"dp": target},
             device_id_type=pl.DeviceIdType.MESH,
         )
 
-    sources = (text_hbm, units.at[IMAGE, 0])
     sent = []
 
     def send(kind, part):
-        copies = [copy(kind, part, sources[kind], 2 * k, peer_dp(2 * k), send_sem) for k in range(1, chips)]
+        copies = [copy(kind, part, 0, 2 * k, peer_dp(2 * k), send_sem) for k in range(1, chips)]
         for c in copies:
             c.start()
         return copies
 
     def send_sibling(kind):
         for part in range(CHUNKS[kind]):
-            sent.append(copy(kind, part, sources[kind], 1, sibling, send_sem))
+            sent.append(copy(kind, part, 0, 1, sibling, send_sem))
             sent[-1].start()
 
     def leave(copies):
@@ -110,22 +107,20 @@
             c.wait_send()
 
     def arrival(kind, part, slot):
-        return copy(kind, part, sources[kind], slot, sibling, send_sem)
+        return copy(kind, part, 0, slot, sibling, send_sem)
 
     def pass_on(kind, part):
         for k in range(1, chips):
             arrival(kind, part, 2 * k).wait_recv()
-            sent.append(copy(kind, part, block(kind, 2 * k), 2 * k + 1, sibling, pass_sem))
+            sent.append(copy(kind, part, 2 * k, 2 * k + 1, sibling, pass_sem))
             sent[-1].start()
 
+    normalize(TEXT)
     pl.semaphore_wait(barrier, n_dp + n_loop - 2)
     texts_out = [c for part in range(CHUNKS[TEXT]) for c in send(TEXT, part)]
     send_sibling(TEXT)
-    loads[IMAGE].wait()
-    norms[IMAGE] = normalize(IMAGE, 0, own_image[...])
+    normalize(IMAGE)
     send_sibling(IMAGE)
-    loads[TEXT].wait()
-    norms[TEXT] = normalize(TEXT, 0, raw[0])
 
     temper = jnp.exp(jnp.full((1, 128), scale_ref[0], jnp.float32))[:, :1]
     offset = bias_ref[0]
@@ -169,20 +164,17 @@
 
     for part in range(CHUNKS[TEXT]):
         arrival(TEXT, part, 1).wait_recv()
-    normalize(TEXT, 1, raw[1])
     total[IMAGE] = row_pair(0, True)
     for part in range(CHUNKS[IMAGE]):
         arrival(IMAGE, part, 1).wait_recv()
     total[TEXT] = col_part(units[IMAGE, 0:2].reshape(2 * rows, -1), True)
     leave(texts_out)
-    images_out = [c for part in range(CHUNKS[IMAGE]) for c in send(IMAGE, part)]
+    images_out = send(IMAGE, 0)
     for part in range(CHUNKS[TEXT]):
         pass_on(TEXT, part)
     for k in range(1, chips):
-        normalize(TEXT, 2 * k, raw[2 * k])
         for part in range(CHUNKS[TEXT]):
             arrival(TEXT, part, 2 * k + 1).wait_recv()
-        normalize(TEXT, 2 * k + 1, raw[2 * k + 1])
         total[IMAGE] += row_pair(k, False)
 
     def exchange(stage, buffer, count, target, axis):
@@ -204,7 +196,9 @@
     )
     dp_copies = exchange(0, dp_sums, n_dp, peer_dp, "dp")
 
-    image_grad_ref[...] = unit_pull(own_image[...], norms[IMAGE], total[IMAGE], temper)
+    leave(images_out)
+    images_out = send(IMAGE, 1)
+    image_grad_ref[...] = unit_pull(own[IMAGE], norms[IMAGE], total[IMAGE], temper)
 
     pass_on(IMAGE, 0)
     for c in dp_copies:
@@ -222,7 +216,7 @@
     for k in range(1, chips):
         arrival(IMAGE, last, 2 * k + 1).wait_recv()
         total[TEXT] += col_part(units[IMAGE, 2 * k + 1, piece(IMAGE, last)], False)
-    text_grad_ref[...] = unit_pull(raw[0], norms[TEXT], total[TEXT], temper)
+    text_grad_ref[...] = unit_pull(own[TEXT], norms[TEXT], total[TEXT], temper)
 
     for c in loop_copies:
         c.wait_recv()
@@ -269,8 +263,7 @@
             in_specs=[hbm, hbm, smem, smem],
             out_specs=(vmem, vmem, vmem),
             scratch_shapes=[
-                pltpu.VMEM((n_dp, rows, width), jnp.bfloat16),
-                pltpu.VMEM((rows, width), jnp.bfloat16),
+                pltpu.VMEM((2, rows, width), jnp.bfloat16),
                 pltpu.VMEM((2, n_dp, rows, width), jnp.bfloat16),
                 pltpu.VMEM((2, rows, width), jnp.float32),
                 pltpu.VMEM((2, rows, 1), jnp.float32),

time: 27.9 us -> 26.6 us (0.953)
  the two profiles are of different devices: /device:TPU:0 before, /device:TPU:1 now
where the time goes in v1:
time: 26.6 us; the launch traced here: 26.4 us
  Pallas kernels  24.5 us (92%)
  between operations  1.93 us (7%)
    pallas_call x1, Pallas kernels, on_device(): pl.pallas_call(functools.partial(kernel, n_dp, n_loop), out_shape=(pltpu....  23.1 us
    pallas_call x1, Pallas kernels, on_device(): pl.pallas_call(functools.partial(finish, 1.0 / (rows * n_dp * n_loop)), o...  1.36 us

profile of v1, /device:TPU:1, one launch (start us, length us, event | category | flops | bytes accessed | tf_op | source)
XLA Modules:
  0.0 26.4 jit_solution(10125130871369208562)
XLA Ops:
  1.9 23.1 %shard_map.83 = (bf16[128,1152]{1,0:T(8,128)(2,1)S(1)}, bf16[128,1152]{1,0:T(8,128)(2,1)S(1)}, f32[8,128]{1,0:T(8,128)S(1)}) custom-call(bf16[128,1152]{1,0:T(8,128)(2,1)} %image_hbm.1, bf16[128,1152]{1,0:T(8,128)(2,1)} %text_hbm.1, f32[1]{0:T(128)S(6)} %copy.9.scale_ref, f32[1]{0:T(128)S(6)} %copy.10.bias_ref), custom_call_target="tpu_custom_call" | custom-call | tf_op jit(solution)/shard_map/pallas_call | solution.py:256
  25.1 1.4 %shard_map.84 = (f32[1]{0:T(128)}, bf16[128,1152]{1,0:T(8,128)(2,1)}, bf16[128,1152]{1,0:T(8,128)(2,1)}, f32[1]{0:T(128)}, f32[1]{0:T(128)}) custom-call(bf16[128,1152]{1,0:T(8,128)(2,1)S(1)} %get-tuple-element.8.image_grad, bf16[128,1152]{1,0:T(8,128)(2,1)S(1)} %get-tuple-element.9.text_grad, f32[8,128]{1,0:T(8,128)S(1)} %get-tuple-element.10.sums_ref), custom_call_target="tpu_custom_call" | custom-call | tf_op jit(solution)/shard_map/pallas_call | solution.py:288

commit v2 on v1

--- a/solution.py
+++ b/solution.py
@@ -55,29 +55,35 @@
     def peer_loop(step):
         return lax.rem(loop + step, n_loop)
 
+    def piece(kind, part):
+        first, last = CUTS[kind][part] * rows // 8, CUTS[kind][part + 1] * rows // 8
+        return pl.ds(first, last - first)
+
+    loads = [
+        [
+            pltpu.make_async_copy(
+                source.at[piece(kind, part)], own.at[kind, piece(kind, part)], load_sem.at[kind, part]
+            )
+            for part in range(CHUNKS[kind])
+        ]
+        for kind, source in ((TEXT, text_hbm), (IMAGE, image_hbm))
+    ]
+    for kind in (TEXT, IMAGE):
+        for load in loads[kind]:
+            load.start()
+
     barrier = pltpu.get_barrier_semaphore()
     for step in range(1, n_dp):
         pl.semaphore_signal(barrier, inc=1, device_id={"dp": peer_dp(step)}, device_id_type=pl.DeviceIdType.MESH)
     for step in range(1, n_loop):
         pl.semaphore_signal(barrier, inc=1, device_id={"loop": peer_loop(step)}, device_id_type=pl.DeviceIdType.MESH)
 
-    loads = [
-        pltpu.make_async_copy(text_hbm, own.at[TEXT], load_sem.at[TEXT]),
-        pltpu.make_async_copy(image_hbm, own.at[IMAGE], load_sem.at[IMAGE]),
-    ]
-    for load in loads:
-        load.start()
-
-    def normalize(kind):
-        loads[kind].wait()
-        floats = own[kind].astype(jnp.float32)
+    def normalize(kind, part):
+        loads[kind][part].wait()
+        floats = own[kind, piece(kind, part)].astype(jnp.float32)
         r = inverse_norm(floats)
-        units[kind, 0] = (floats * r).astype(jnp.bfloat16)
-        norms[kind] = r
-
-    def piece(kind, part):
-        first, last = CUTS[kind][part] * rows // 8, CUTS[kind][part + 1] * rows // 8
-        return pl.ds(first, last - first)
+        units[kind, 0, piece(kind, part)] = (floats * r).astype(jnp.bfloat16)
+        norms[kind, piece(kind, part)] = r
 
     def copy(kind, part, from_slot, to_slot, target, sem):
         return pltpu.make_async_remote_copy(
@@ -115,11 +121,15 @@
             sent.append(copy(kind, part, 2 * k, 2 * k + 1, sibling, pass_sem))
             sent[-1].start()
 
-    normalize(TEXT)
-    pl.semaphore_wait(barrier, n_dp + n_loop - 2)
-    texts_out = [c for part in range(CHUNKS[TEXT]) for c in send(TEXT, part)]
+    texts_out = []
+    for part in range(CHUNKS[TEXT]):
+        normalize(TEXT, part)
+        if part == 0:
+            pl.semaphore_wait(barrier, n_dp + n_loop - 2)
+        texts_out += send(TEXT, part)
     send_sibling(TEXT)
-    normalize(IMAGE)
+    for part in range(CHUNKS[IMAGE]):
+        normalize(IMAGE, part)
     send_sibling(IMAGE)
 
     temper = jnp.exp(jnp.full((1, 128), scale_ref[0], jnp.float32))[:, :1]
@@ -227,7 +237,7 @@
 
 def finish(
     inverse_batch, image_grad, text_grad, sums_ref,
-    loss_ref, image_grad_hbm, text_grad_hbm, scale_grad_ref, bias_grad_ref, sems,
+    loss_hbm, image_grad_hbm, text_grad_hbm, scale_grad_hbm, bias_grad_hbm, scalars, sems,
 ):
     stores = [
         pltpu.make_async_copy(image_grad, image_grad_hbm, sems.at[0]),
@@ -235,9 +245,11 @@
     ]
     for store in stores:
         store.start()
-    loss_ref[0] = jnp.sum(sums_ref[0:1, :]) * inverse_batch
-    scale_grad_ref[0] = jnp.sum(sums_ref[1:2, :])
-    bias_grad_ref[0] = jnp.sum(sums_ref[2:3, :])
+    totals = jnp.sum(sums_ref[...], axis=1, keepdims=True)
+    for i, (target, factor) in enumerate(((loss_hbm, inverse_batch), (scale_grad_hbm, 1.0), (bias_grad_hbm, 1.0))):
+        scalars[i, 0] = totals[i, 0] * factor
+        stores.append(pltpu.make_async_copy(scalars.at[i], target, sems.at[2 + i]))
+        stores[-1].start()
     for store in stores:
         store.wait()
 
@@ -269,7 +281,7 @@
                 pltpu.VMEM((2, rows, 1), jnp.float32),
                 pltpu.VMEM((n_dp, 8, 128), jnp.float32),
                 pltpu.VMEM((n_loop, 8, 128), jnp.float32),
-                pltpu.SemaphoreType.DMA((2,)),
+                pltpu.SemaphoreType.DMA((2, parts)),
                 pltpu.SemaphoreType.DMA((2, n_dp, parts)),
                 pltpu.SemaphoreType.DMA((2, n_dp, parts)),
                 pltpu.SemaphoreType.DMA((2, n_dp, parts)),
@@ -289,8 +301,8 @@
             functools.partial(finish, 1.0 / (rows * n_dp * n_loop)),
             out_shape=(scalar, grad, grad, scalar, scalar),
             in_specs=[vmem] * 3,
-            out_specs=(smem, hbm, hbm, smem, smem),
-            scratch_shapes=[pltpu.SemaphoreType.DMA((2,))],
+            out_specs=(hbm, hbm, hbm, hbm, hbm),
+            scratch_shapes=[pltpu.SMEM((3, 1), jnp.float32), pltpu.SemaphoreType.DMA((5,))],
             compiler_params=pltpu.CompilerParams(vmem_limit_bytes=4 * 1024 * 1024),
         )(image_grad, text_grad, sums)
 

time: 26.6 us -> 26.1 us (0.981)
  Pallas kernels: 24.5 us -> 24 us
    pallas_call x1, Pallas kernels: 1.36 us -> 0.88 us  [on_device(): pl.pallas_call(functools.partial(finish, 1.0 / (rows * n_dp * n_loop)), o...]
where the time goes in v2:
time: 26.1 us; the launch traced here: 26 us
  Pallas kernels  24 us (92%)
  between operations  1.93 us (7%)
    pallas_call x1, Pallas kernels, on_device(): pl.pallas_call(functools.partial(kernel, n_dp, n_loop), out_shape=(pltpu....  23.2 us
    pallas_call x1, Pallas kernels, on_device(): pl.pallas_call(functools.partial(finish, 1.0 / (rows * n_dp * n_loop)), o...  0.88 us

profile of v2, /device:TPU:1, one launch (start us, length us, event | category | flops | bytes accessed | tf_op | source)
XLA Modules:
  0.0 26.0 jit_solution(12294174831563221129)
XLA Ops:
  1.9 23.2 %shard_map.83 = (bf16[128,1152]{1,0:T(8,128)(2,1)S(1)}, bf16[128,1152]{1,0:T(8,128)(2,1)S(1)}, f32[8,128]{1,0:T(8,128)S(1)}) custom-call(bf16[128,1152]{1,0:T(8,128)(2,1)} %image_hbm.1, bf16[128,1152]{1,0:T(8,128)(2,1)} %text_hbm.1, f32[1]{0:T(128)S(6)} %copy.9.scale_ref, f32[1]{0:T(128)S(6)} %copy.10.bias_ref), custom_call_target="tpu_custom_call" | custom-call | tf_op jit(solution)/shard_map/pallas_call | solution.py:268
  25.1 0.9 %shard_map.84 = (f32[1]{0:T(128)}, bf16[128,1152]{1,0:T(8,128)(2,1)}, bf16[128,1152]{1,0:T(8,128)(2,1)}, f32[1]{0:T(128)}, f32[1]{0:T(128)}) custom-call(bf16[128,1152]{1,0:T(8,128)(2,1)S(1)} %get-tuple-element.8.image_grad, bf16[128,1152]{1,0:T(8,128)(2,1)S(1)} %get-tuple-element.9.text_grad, f32[8,128]{1,0:T(8,128)S(1)} %get-tuple-element.10.sums_ref), custom_call_target="tpu_custom_call" | custom-call | tf_op jit(solution)/shard_map/pallas_call | solution.py:300

commit v3 on v2

--- a/solution.py
+++ b/solution.py
@@ -59,6 +59,12 @@
         first, last = CUTS[kind][part] * rows // 8, CUTS[kind][part + 1] * rows // 8
         return pl.ds(first, last - first)
 
+    barrier = pltpu.get_barrier_semaphore()
+    for step in range(1, n_dp):
+        pl.semaphore_signal(barrier, inc=1, device_id={"dp": peer_dp(step)}, device_id_type=pl.DeviceIdType.MESH)
+    for step in range(1, n_loop):
+        pl.semaphore_signal(barrier, inc=1, device_id={"loop": peer_loop(step)}, device_id_type=pl.DeviceIdType.MESH)
+
     loads = [
         [
             pltpu.make_async_copy(
@@ -72,12 +78,6 @@
         for load in loads[kind]:
             load.start()
 
-    barrier = pltpu.get_barrier_semaphore()
-    for step in range(1, n_dp):
-        pl.semaphore_signal(barrier, inc=1, device_id={"dp": peer_dp(step)}, device_id_type=pl.DeviceIdType.MESH)
-    for step in range(1, n_loop):
-        pl.semaphore_signal(barrier, inc=1, device_id={"loop": peer_loop(step)}, device_id_type=pl.DeviceIdType.MESH)
-
     def normalize(kind, part):
         loads[kind][part].wait()
         floats = own[kind, piece(kind, part)].astype(jnp.float32)
@@ -150,8 +150,7 @@
         wide = jnp.concatenate([eye(), jnp.zeros((rows, rows), jnp.bool_)], axis=1)
         return jnp.where(wide, values - subtrahend, values)
 
-    def row_pair(k, first):
-        texts = units[TEXT, 2 * k:2 * k + 2].reshape(2 * rows, -1)
+    def row_part(texts, first):
         scaled = temper * dot_nt(image_unit, texts)
         logits = scaled + offset
         losses, coef = softplus_and_sigmoid(logits)
@@ -169,12 +168,9 @@
             coef = less_eye(coef, 1.0)
         return jnp.dot(coef.astype(jnp.bfloat16), images, preferred_element_type=jnp.float32)
 
-    def image_pair(k, part):
-        return units[IMAGE, 2 * k:2 * k + 2, piece(IMAGE, part)].reshape(-1, units.shape[3])
-
     for part in range(CHUNKS[TEXT]):
         arrival(TEXT, part, 1).wait_recv()
-    total[IMAGE] = row_pair(0, True)
+    total[IMAGE] = row_part(units[TEXT, 0:2].reshape(2 * rows, -1), True)
     for part in range(CHUNKS[IMAGE]):
         arrival(IMAGE, part, 1).wait_recv()
     total[TEXT] = col_part(units[IMAGE, 0:2].reshape(2 * rows, -1), True)
@@ -183,9 +179,13 @@
     for part in range(CHUNKS[TEXT]):
         pass_on(TEXT, part)
     for k in range(1, chips):
+        total[IMAGE] += row_part(units[TEXT, 2 * k], False)
+    for k in range(1, chips):
         for part in range(CHUNKS[TEXT]):
             arrival(TEXT, part, 2 * k + 1).wait_recv()
-        total[IMAGE] += row_pair(k, False)
+        total[IMAGE] += row_part(units[TEXT, 2 * k + 1], False)
+    leave(images_out)
+    images_out = send(IMAGE, 1)
 
     def exchange(stage, buffer, count, target, axis):
         copies = []
@@ -206,8 +206,6 @@
     )
     dp_copies = exchange(0, dp_sums, n_dp, peer_dp, "dp")
 
-    leave(images_out)
-    images_out = send(IMAGE, 1)
     image_grad_ref[...] = unit_pull(own[IMAGE], norms[IMAGE], total[IMAGE], temper)
 
     pass_on(IMAGE, 0)
@@ -215,17 +213,14 @@
         c.wait_recv()
     loop_sums[0] = jnp.sum(dp_sums[...], axis=0)
     loop_copies = exchange(1, loop_sums, n_loop, peer_loop, "loop")
-    for part in range(CHUNKS[IMAGE] - 1):
+    for part in range(CHUNKS[IMAGE]):
+        if part:
+            pass_on(IMAGE, part)
+        for k in range(1, chips):
+            total[TEXT] += col_part(units[IMAGE, 2 * k, piece(IMAGE, part)], False)
         for k in range(1, chips):
             arrival(IMAGE, part, 2 * k + 1).wait_recv()
-            total[TEXT] += col_part(image_pair(k, part), False)
-        pass_on(IMAGE, part + 1)
-    last = CHUNKS[IMAGE] - 1
-    for k in range(1, chips):
-        total[TEXT] += col_part(units[IMAGE, 2 * k, piece(IMAGE, last)], False)
-    for k in range(1, chips):
-        arrival(IMAGE, last, 2 * k + 1).wait_recv()
-        total[TEXT] += col_part(units[IMAGE, 2 * k + 1, piece(IMAGE, last)], False)
+            total[TEXT] += col_part(units[IMAGE, 2 * k + 1, piece(IMAGE, part)], False)
     text_grad_ref[...] = unit_pull(own[TEXT], norms[TEXT], total[TEXT], temper)
 
     for c in loop_copies:

time: 26.1 us -> 27.6 us (1.057)
  the two profiles are of different devices: /device:TPU:1 before, /device:TPU:0 now
where the time goes in v3:
time: 27.6 us; the launch traced here: 27.4 us
  Pallas kernels  25.5 us (92%)
  between operations  1.93 us (7%)
    pallas_call x1, Pallas kernels, on_device(): pl.pallas_call(functools.partial(kernel, n_dp, n_loop), out_shape=(pltpu....  24.6 us
    pallas_call x1, Pallas kernels, on_device(): pl.pallas_call(functools.partial(finish, 1.0 / (rows * n_dp * n_loop)), o...  0.88 us

profile of v3, /device:TPU:0, one launch (start us, length us, event | category | flops | bytes accessed | tf_op | source)
XLA Modules:
  0.0 27.4 jit_solution(5904383524486467722)
XLA Ops:
  1.9 24.6 %shard_map.83 = (bf16[128,1152]{1,0:T(8,128)(2,1)S(1)}, bf16[128,1152]{1,0:T(8,128)(2,1)S(1)}, f32[8,128]{1,0:T(8,128)S(1)}) custom-call(bf16[128,1152]{1,0:T(8,128)(2,1)} %image_hbm.1, bf16[128,1152]{1,0:T(8,128)(2,1)} %text_hbm.1, f32[1]{0:T(128)S(6)} %copy.9.scale_ref, f32[1]{0:T(128)S(6)} %copy.10.bias_ref), custom_call_target="tpu_custom_call" | custom-call | tf_op jit(solution)/shard_map/pallas_call | solution.py:263
  26.5 0.9 %shard_map.84 = (f32[1]{0:T(128)}, bf16[128,1152]{1,0:T(8,128)(2,1)}, bf16[128,1152]{1,0:T(8,128)(2,1)}, f32[1]{0:T(128)}, f32[1]{0:T(128)}) custom-call(bf16[128,1152]{1,0:T(8,128)(2,1)S(1)} %get-tuple-element.8.image_grad, bf16[128,1152]{1,0:T(8,128)(2,1)S(1)} %get-tuple-element.9.text_grad, f32[8,128]{1,0:T(8,128)S(1)} %get-tuple-element.10.sums_ref), custom_call_target="tpu_custom_call" | custom-call | tf_op jit(solution)/shard_map/pallas_call | solution.py:295

commit v4 on v2

--- a/solution.py
+++ b/solution.py
@@ -215,17 +215,12 @@
         c.wait_recv()
     loop_sums[0] = jnp.sum(dp_sums[...], axis=0)
     loop_copies = exchange(1, loop_sums, n_loop, peer_loop, "loop")
-    for part in range(CHUNKS[IMAGE] - 1):
+    for part in range(CHUNKS[IMAGE]):
+        if part:
+            pass_on(IMAGE, part)
         for k in range(1, chips):
             arrival(IMAGE, part, 2 * k + 1).wait_recv()
             total[TEXT] += col_part(image_pair(k, part), False)
-        pass_on(IMAGE, part + 1)
-    last = CHUNKS[IMAGE] - 1
-    for k in range(1, chips):
-        total[TEXT] += col_part(units[IMAGE, 2 * k, piece(IMAGE, last)], False)
-    for k in range(1, chips):
-        arrival(IMAGE, last, 2 * k + 1).wait_recv()
-        total[TEXT] += col_part(units[IMAGE, 2 * k + 1, piece(IMAGE, last)], False)
     text_grad_ref[...] = unit_pull(own[TEXT], norms[TEXT], total[TEXT], temper)
 
     for c in loop_copies:

time: 26.1 us -> 26.1 us (level)
  no operation moved by 1% of the time
where the time goes in v4:
time: 26.1 us; the launch traced here: 26 us
  Pallas kernels  24 us (92%)
  between operations  1.93 us (7%)
    pallas_call x1, Pallas kernels, on_device(): pl.pallas_call(functools.partial(kernel, n_dp, n_loop), out_shape=(pltpu....  23.1 us
    pallas_call x1, Pallas kernels, on_device(): pl.pallas_call(functools.partial(finish, 1.0 / (rows * n_dp * n_loop)), o...  0.88 us

profile of v4, /device:TPU:1, one launch (start us, length us, event | category | flops | bytes accessed | tf_op | source)
XLA Modules:
  0.0 26.0 jit_solution(15486605505595234995)
XLA Ops:
  1.9 23.1 %shard_map.83 = (bf16[128,1152]{1,0:T(8,128)(2,1)S(1)}, bf16[128,1152]{1,0:T(8,128)(2,1)S(1)}, f32[8,128]{1,0:T(8,128)S(1)}) custom-call(bf16[128,1152]{1,0:T(8,128)(2,1)} %image_hbm.1, bf16[128,1152]{1,0:T(8,128)(2,1)} %text_hbm.1, f32[1]{0:T(128)S(6)} %copy.9.scale_ref, f32[1]{0:T(128)S(6)} %copy.10.bias_ref), custom_call_target="tpu_custom_call" | custom-call | tf_op jit(solution)/shard_map/pallas_call | solution.py:263
  25.1 0.9 %shard_map.84 = (f32[1]{0:T(128)}, bf16[128,1152]{1,0:T(8,128)(2,1)}, bf16[128,1152]{1,0:T(8,128)(2,1)}, f32[1]{0:T(128)}, f32[1]{0:T(128)}) custom-call(bf16[128,1152]{1,0:T(8,128)(2,1)S(1)} %get-tuple-element.8.image_grad, bf16[128,1152]{1,0:T(8,128)(2,1)S(1)} %get-tuple-element.9.text_grad, f32[8,128]{1,0:T(8,128)S(1)} %get-tuple-element.10.sums_ref), custom_call_target="tpu_custom_call" | custom-call | tf_op jit(solution)/shard_map/pallas_call | solution.py:295
